TPU v7x, 32 devices: a whole 2x2x4 slice. The times are simulated.
32 devices in a mesh: grp: 4 (over y, x), orient: 8 (over z, core).
Axes of the slice: x: 2, y: 2, z: 4, core: 2. Of those that a mesh axis runs over, the one named last changes fastest.
Arguments:
- images: bfloat16 [1024, 2, 8192], P(('grp', 'orient')), may hold values from -6 to 6
- ctf: bfloat16 [1024, 8192], P(('grp', 'orient')), may hold values from -1 to 1
- shifts: int32 [1024, 2], P(('grp', 'orient')), may hold values from -8 to 8
- home: int32 [4, 1024, 1], P(None, ('grp', 'orient')), may hold values from 0 to 7; in each aligned block of 32 rows (0 to 31, 32 to 63, ..., all dimensions but the last counted through in order) at most 8 rows name the same one
- neighbours: int32 [1024, 4, 128], P(('grp', 'orient')), may hold values from 0 to 511
- references: bfloat16 [4, 4096, 2, 8192], P('grp', 'orient'), may hold values from -6 to 6
- noise_weight: float32 [4, 8192], P('grp'), may hold values from 0.25 to 4
Outputs:
- centred: float32 [1024, 4, 128], P(('grp', 'orient'))
Inputs may be any that keep to these rules, and one draw needn't show every extreme that they name: `home`: within one group, at most 8 of the 32 particles of one device share a block, and in every draw some device has exactly 8 particles in one block.
All inputs are finite; a program needn't handle non-finite values.
Results may differ from a plain program's by a relative error of at most 0.0042.
Values may be sent and summed in bfloat16 or wider, within the bound.
A program may use at most 256 MiB of HBM per device.

v0:
```python
import math

import jax
import jax.numpy as jnp
from jax import lax
from jax.sharding import PartitionSpec as P

BOX = 128
PIX = 8192


def shift_tables(shifts, box):
    half = box // 2
    row = jnp.arange(box, dtype=jnp.int32)
    freq_y = jnp.where(row < half, row, row - box).astype(jnp.float32)
    freq_x = jnp.arange(half, dtype=jnp.int32).astype(jnp.float32)
    grid_y = jnp.broadcast_to(freq_y[:, None], (box, half)).reshape(-1)
    grid_x = jnp.broadcast_to(freq_x[None, :], (box, half)).reshape(-1)
    move_x = shifts[:, 0].astype(jnp.float32)
    move_y = shifts[:, 1].astype(jnp.float32)
    angle = (
        -2.0
        * math.pi
        / box
        * (move_x[:, None] * grid_x[None, :] + move_y[:, None] * grid_y[None, :])
    )
    return (jnp.cos(angle), jnp.sin(angle))


def pick_columns(table, lists):
    width = table.shape[-1]
    marks = (lists[..., None] == jnp.arange(width, dtype=jnp.int32)).astype(jnp.float32)
    return jnp.einsum("ano,ao->an", marks, table, precision=lax.Precision.HIGHEST)


def per_device(images, ctf, shifts, home, neighbours, references, noise_weight):
    groups = home.shape[0]
    owners = lax.axis_size("orient")
    devices = groups * owners
    local = images.shape[0]
    pixels = images.shape[2]
    slots = max(2, 2 * local // owners)
    cosine, sine = shift_tables(shifts, BOX)
    real = images[:, 0].astype(jnp.float32)
    imag = images[:, 1].astype(jnp.float32)
    payload = jnp.stack(
        [real * cosine - imag * sine, real * sine + imag * cosine, ctf.astype(jnp.float32)], axis=1
    ).astype(jnp.bfloat16)
    target = home[:, :, 0]
    places = jnp.arange(owners, dtype=jnp.int32)
    hits = (target[:, :, None] == places[None, None, :]).astype(jnp.int32)
    rank = jnp.sum((jnp.cumsum(hits, axis=1) - hits) * hits, axis=2)
    slot = (jnp.arange(groups, dtype=jnp.int32)[:, None] * owners + target) * slots + rank
    total = devices * slots
    chosen = (slot[:, None, :] == jnp.arange(total, dtype=jnp.int32)[None, :, None]).astype(
        jnp.int32
    )
    select = jnp.sum(chosen, axis=0).astype(jnp.bfloat16)
    buffer = jnp.dot(select, payload.reshape(local, -1), preferred_element_type=jnp.float32).astype(
        jnp.bfloat16
    )
    buffer = buffer.reshape(devices, slots, 3, pixels)
    weight = noise_weight[0]
    blocks = references[0]
    flat_refs = blocks.reshape(blocks.shape[0], -1)
    ref_real = blocks[:, 0].astype(jnp.float32)
    ref_imag = blocks[:, 1].astype(jnp.float32)
    ref_power = (ref_real * ref_real + ref_imag * ref_imag).astype(jnp.bfloat16)
    scale = 1.0 / math.sqrt(PIX)
    contract = (((1,), (1,)), ((), ()))
    arrived = lax.all_to_all(buffer, ("grp", "orient"), split_axis=0, concat_axis=0, tiled=True)
    lead = arrived.shape[:2]
    flat = arrived.reshape(-1, 3, pixels).astype(jnp.float32)
    tone = weight[None, :] * flat[:, 2]
    weighted = (tone[:, None, :] * flat[:, :2]).astype(jnp.bfloat16).reshape(flat.shape[0], -1)
    tone_power = (tone * flat[:, 2]).astype(jnp.bfloat16)
    cross = lax.dot_general(weighted, flat_refs, contract, preferred_element_type=jnp.float32)
    power = lax.dot_general(tone_power, ref_power, contract, preferred_element_type=jnp.float32)
    table = ((power - 2.0 * cross) * scale).reshape(lead + (-1,))
    returned = lax.all_to_all(table, ("grp", "orient"), split_axis=0, concat_axis=0, tiled=True)
    flat_back = returned.reshape(total, -1)
    mine = jnp.einsum(
        "gsp,sk->pgk", chosen.astype(jnp.float32), flat_back, precision=lax.Precision.HIGHEST
    )
    mine = pick_columns(
        mine.reshape(local * groups, -1), neighbours.reshape(local * groups, -1)
    ).reshape(local, groups, -1)
    return mine - jnp.mean(mine, axis=2, keepdims=True)


def solution(mesh):
    in_specs = (
        P(("grp", "orient"), None, None),
        P(("grp", "orient"), None),
        P(("grp", "orient"), None),
        P(None, ("grp", "orient"), None),
        P(("grp", "orient"), None, None),
        P("grp", "orient", None, None),
        P("grp", None),
    )
    out_specs = P(("grp", "orient"), None, None)
    return jax.shard_map(
        per_device, mesh=mesh, in_specs=in_specs, out_specs=out_specs, check_vma=False
    )
```

profile of v0, /device:TPU:0, one launch (start us, length us, event | category | flops | bytes accessed | tf_op | source)
XLA Modules:
  0.0 398.5 jit_solution(2978858096762238727)
XLA Ops:
  0.0 3.6 fusion.38
  3.6 0.8 convert_bitcast_fusion.1
  4.6 4.8 %fusion.28 = (bf16[32,1,8192]{2,0,1:T(8,128)(2,1)S(1)}, bf16[32,1,8192]{2,0,1:T(8,128)(2,1)S(1)}) fusion(f32[8192]{0:T(1024)S(1)} %mul.160, f32[32]{0:T(128)S(1)} %get-tuple-element.10, f32[8192]{0:T(1024)S(1)} %mul.156, f32[32]{0:T(128)S(1)} %get-tuple-element.9, bf16[32,1,8192]{2,1,0:T(2,128)(2,1)S(1)} %get-tuple-element.8, ...), kind=kLoop, calls=%fused_computation.28 | loop fusion | flops 3670016 | bytes 2162944 | tf_op jit(solution)/shard_map/convert.2
  9.4 1.2 maximum_bitcast_fusion
  10.9 0.2 select_reduce_fusion
  11.3 6.3 %convolution_convert_fusion = bf16[256,24576]{1,0:T(8,128)(2,1)} fusion(bf16[32,24576]{1,0:T(8,128)(2,1)S(1)} %bitcast.67, s32[256,32]{0,1:T(8,128)S(1)} %convert_reduce_fusion), kind=kOutput, calls=%fused_computation.2 | convolution fusion | flops 408952832 | bytes 14188544 | tf_op jit(solution)/shard_map/dot_general | solution.py:59
  17.6 7.6 %all-to-all-start = ((bf16[32,8,3,8192]{3,1,2,0:T(8,128)(2,1)}), bf16[32,8,3,8192]{3,1,2,0:T(8,128)(2,1)}, u32[]{:S(2)}, u32[]{:S(2)}) async-start(bf16[32,8,3,8192]{3,1,2,0:T(8,128)(2,1)} %bitcast.63), calls=%async_computation | async-start | bytes 25165824 | tf_op jit(solution)/shard_map/all_to_all | solution.py:71
  25.2 18.5 %copy.42 = bf16[1,512,2,8192]{3,1,2,0:T(8,128)(2,1)} copy(bf16[1,512,2,8192]{3,2,1,0:T(2,128)(2,1)} %param.12) | data formatting | bytes 33554432 | tf_op args[5]
  43.7 18.5 %copy.35 = bf16[64,8,2,8192]{3,1,2,0:T(8,128)(2,1)} copy(bf16[64,8,2,8192]{3,2,1,0:T(2,128)(2,1)} %bitcast.62) | data formatting | bytes 33554432
  62.2 237.6 %all-to-all-done = bf16[32,8,3,8192]{3,1,2,0:T(8,128)(2,1)} async-done(((bf16[32,8,3,8192]{3,1,2,0:T(8,128)(2,1)}), bf16[32,8,3,8192]{3,1,2,0:T(8,128)(2,1)}, u32[]{:S(2)}, u32[]{:S(2)}) %all-to-all-start) | async-done | bytes 12582944 | tf_op jit(solution)/shard_map/all_to_all | solution.py:71
  299.9 14.2 %bitcast_convert_fusion = f32[256,3,8192]{2,0,1:T(8,128)} fusion(bf16[32,8,3,8192]{3,1,2,0:T(8,128)(2,1)} %all-to-all-done), kind=kLoop, calls=%fused_computation.8 | loop fusion | flops 6291456 | bytes 37748736 | tf_op jit(solution)/shard_map/convert_element_type | solution.py:73
  314.0 4.3 %multiply_bitcast_fusion = f32[256,8192]{1,0:T(8,128)S(1)} fusion(f32[256,3,8192]{2,0,1:T(8,128)} %bitcast_convert_fusion, f32[8192]{0:T(1024)S(1)} %bitcast.73), kind=kLoop, calls=%fused_computation.9 | loop fusion | flops 2097152 | bytes 16809984 | tf_op jit(solution)/shard_map/mul | solution.py:75
  318.3 9.3 %fusion.1 = bf16[256,2,8192]{2,0,1:T(8,128)(2,1)} fusion(f32[256,3,8192]{2,0,1:T(8,128)} %bitcast_convert_fusion, f32[256,8192]{1,0:T(8,128)S(1)} %multiply_bitcast_fusion), kind=kLoop, calls=%fused_computation.4 | loop fusion | flops 8388608 | bytes 33554432 | tf_op jit(solution)/shard_map/convert_element_type | solution.py:75
  327.6 11.9 %copy.28 = bf16[256,2,8192]{0,2,1:T(8,128)(2,1)} copy(bf16[256,2,8192]{2,0,1:T(8,128)(2,1)} %fusion.1) | data formatting | bytes 16777216 | tf_op jit(solution)/shard_map/convert_element_type | solution.py:75
  339.5 10.6 %convolution_multiply_fusion = f32[256,512]{1,0:T(8,128)S(1)} fusion(bf16[256,16384]{0,1:T(8,128)(2,1)} %bitcast.66, bf16[512,16384]{1,0:T(8,128)(2,1)} %bitcast.65), kind=kOutput, calls=%fused_computation.23 | convolution fusion | flops 4295098368 | bytes 25690112 | tf_op jit(solution)/shard_map/dot_general | solution.py:77
  350.1 11.3 %fusion.22 = f32[32,8,512]{2,1,0:T(8,128)} fusion(f32[256,512]{1,0:T(8,128)S(1)} %convolution_multiply_fusion, bf16[512,2,8192]{2,0,1:T(8,128)(2,1)} %bitcast.64, f32[256,3,8192]{2,0,1:T(8,128)} %bitcast_convert_fusion, f32[8192]{0:T(1024)S(1)} %bitcast.74), kind=kOutput, calls=%fused_computation.26 | convolution fusion | flops 2179203072 | bytes 26247168 | tf_op jit(solution)/shard_map/dot_general | solution.py:78
  361.5 2.8 all-to-all-start.1
  364.4 16.0 %all-to-all-done.1 = f32[32,8,512]{2,1,0:T(8,128)S(1)} async-done(((f32[32,8,512]{2,1,0:T(8,128)}), f32[32,8,512]{2,1,0:T(8,128)S(1)}, u32[]{:S(2)}, u32[]{:S(2)}) %all-to-all-start.1) | async-done | bytes 524320 | tf_op jit(solution)/shard_map/all_to_all | solution.py:80
  380.4 0.4 fusion.33
  380.9 0.2 copy.29
  381.1 0.4 reshape.327
  381.4 16.1 %fusion = f32[128,1,128]{2,1,0:T(1,128)S(1)} fusion(f32[128,512,1]{1,2,0:T(1,128)S(1)} %reshape.327, s32[128,128]{1,0:T(8,128)S(1)} %bitcast.78), kind=kOutput, calls=%fused_computation.1 | convolution fusion | flops 109051904 | bytes 393216 | tf_op jit(solution)/shard_map/ano,ao->an/dot_general | solution.py:33
  397.5 0.1 reduce_sum.29
  397.8 0.7 broadcast_subtract_fusion
  (21 shorter events, 0.9 us)
Async XLA Ops:
  0.0 10.7 %copy-start.1 = (s32[4,32,1]{1,2,0:T(1,128)S(1)}, s32[4,32,1]{1,2,0:T(1,128)}, u32[]{:S(2)}) copy-start(s32[4,32,1]{1,2,0:T(1,128)} %param.10) | copy-start | bytes 1540
  17.6 282.2 %all-to-all-start = ((bf16[32,8,3,8192]{3,1,2,0:T(8,128)(2,1)}), bf16[32,8,3,8192]{3,1,2,0:T(8,128)(2,1)}, u32[]{:S(2)}, u32[]{:S(2)}) async-start(bf16[32,8,3,8192]{3,1,2,0:T(8,128)(2,1)} %bitcast.63), calls=%async_computation | async-start | bytes 25165824 | tf_op jit(solution)/shard_map/all_to_all | solution.py:71
  62.2 251.8 %copy-start = (f32[1,8192]{1,0:T(1,128)S(1)}, f32[1,8192]{1,0:T(1,128)}, u32[]{:S(2)}) copy-start(f32[1,8192]{1,0:T(1,128)} %param.13) | copy-start | bytes 98308
  350.1 31.3 %copy-start.2 = (s32[32,4,128]{2,1,0:T(4,128)S(1)}, s32[32,4,128]{2,1,0:T(4,128)}, u32[]{:S(2)}) copy-start(s32[32,4,128]{2,1,0:T(4,128)} %param.11) | copy-start | bytes 196612
  361.5 19.0 %all-to-all-start.1 = ((f32[32,8,512]{2,1,0:T(8,128)}), f32[32,8,512]{2,1,0:T(8,128)S(1)}, u32[]{:S(2)}, u32[]{:S(2)}) async-start(f32[32,8,512]{2,1,0:T(8,128)} %fusion.22), calls=%async_computation.1 | async-start | bytes 1048576 | tf_op jit(solution)/shard_map/all_to_all | solution.py:80
where the time goes:
time: 400 us; the launch traced here: 399 us
  waiting for transfers between devices  254 us (64%)
  local copies, waits for them, and re-layouts  53.5 us (13%)
  matrix products  44.8 us (11%)
  other arithmetic  35.9 us (9%)
  starting transfers between devices  10.4 us (3%)
    all_to_all x1, waiting for transfers between devices, per_device(): lax.all_to_all(buffer, ('grp', 'orient'), split_axis=0, concat_axis=0, ti...  238 us
    unnamed x8, local copies, waits for them, and re-layouts  37 us
    dot_general x1, matrix products, pick_columns(): jnp.einsum('ano,ao->an', marks, table, precision=lax.Precision.HIGHEST)  16.1 us
    all_to_all x1, waiting for transfers between devices, per_device(): lax.all_to_all(table, ('grp', 'orient'), split_axis=0, concat_axis=0, til...  16 us
    convert_element_type x1, other arithmetic, per_device(): flat = arrived.reshape(-1, 3, pixels).astype(jnp.float32)  14.2 us
    convert_element_type x1, local copies, waits for them, and re-layouts, per_device(): (tone[:, None, :] * flat[:, :2]).astype(jnp.bfloat16)  11.9 us
    dot_general x1, matrix products, per_device(): lax.dot_general(tone_power, ref_power, contract, preferred_element_type=j...  11.3 us
    dot_general x1, matrix products, per_device(): lax.dot_general(weighted, flat_refs, contract, preferred_element_type=jnp...  10.6 us
  transfers between devices with their start and end apart: 2, of which 2 were waited for; matrix products, arithmetic and copies ran while one was open for 9% of the time, Pallas kernels for 0%

commit v1 on v0

--- a/solution.py
+++ b/solution.py
@@ -1,8 +1,11 @@
+import functools
 import math
 
 import jax
 import jax.numpy as jnp
 from jax import lax
+from jax.experimental import pallas as pl
+from jax.experimental.pallas import tpu as pltpu
 from jax.sharding import PartitionSpec as P
 
 BOX = 128
@@ -33,7 +36,7 @@
     return jnp.einsum("ano,ao->an", marks, table, precision=lax.Precision.HIGHEST)
 
 
-def per_device(images, ctf, shifts, home, neighbours, references, noise_weight):
+def per_device_plain(images, ctf, shifts, home, neighbours, references, noise_weight):
     groups = home.shape[0]
     owners = lax.axis_size("orient")
     devices = groups * owners
@@ -88,6 +91,353 @@
     return mine - jnp.mean(mine, axis=2, keepdims=True)
 
 
+MESH = pl.DeviceIdType.MESH
+CHUNKS = 4
+
+
+def route_kernel(groups, columns, marks_ref, own_ref, out_ref, pool, marks, packed,
+                 own_sem, mate_send, mate_recv, mark_send, mark_recv,
+                 line_send, line_recv, move_send, move_recv):
+    grp = lax.axis_index("grp")
+    orient = lax.axis_index("orient")
+    place, core = orient // 2, orient % 2
+    local = own_ref.shape[0]
+    half = own_ref.shape[1] // 2
+    span = half // CHUNKS
+    rows = out_ref.shape[0] // (groups * columns)
+    tile = min(1024, span)
+
+    barrier = pltpu.get_barrier_semaphore()
+    for step in range(1, 2 * columns):
+        pl.semaphore_signal(barrier, inc=1, device_id=(grp, (orient + step) % (2 * columns)), device_id_type=MESH)
+    for step in range(1, groups):
+        for side in range(2):
+            pl.semaphore_signal(
+                barrier, inc=1, device_id=((grp + step) % groups, 2 * place + side), device_id_type=MESH
+            )
+    pl.semaphore_wait(barrier, 2 * columns - 1 + 2 * (groups - 1))
+
+    def cols(chunk):
+        return pl.ds(pl.multiple_of(chunk * span, 128), span)
+
+    def mark_copy(step):
+        return pltpu.make_async_remote_copy(
+            src_ref=marks_ref, dst_ref=marks.at[orient],
+            send_sem=mark_send.at[step], recv_sem=mark_recv.at[orient],
+            device_id=(grp, (orient + step) % (2 * columns)), device_id_type=MESH)
+
+    def mark_arrival(source):
+        return pltpu.make_async_remote_copy(
+            src_ref=marks_ref, dst_ref=marks.at[source],
+            send_sem=mark_send.at[0], recv_sem=mark_recv.at[source],
+            device_id=(grp, (orient + 1) % (2 * columns)), device_id_type=MESH)
+
+    def own_copy(chunk):
+        return pltpu.make_async_copy(
+            own_ref.at[:, pl.ds(pl.multiple_of(core * half + chunk * span, 128), span)],
+            pool.at[place, pl.ds(pl.multiple_of(core * local, 16), local), cols(chunk)],
+            own_sem.at[chunk])
+
+    def mate_copy(chunk):
+        return pltpu.make_async_remote_copy(
+            src_ref=own_ref.at[:, pl.ds(pl.multiple_of((1 - core) * half + chunk * span, 128), span)],
+            dst_ref=pool.at[place, pl.ds(pl.multiple_of(core * local, 16), local), cols(chunk)],
+            send_sem=mate_send.at[chunk], recv_sem=mate_recv.at[chunk],
+            device_id=(grp, 2 * place + 1 - core), device_id_type=MESH)
+
+    def mate_arrival(chunk):
+        return pltpu.make_async_remote_copy(
+            src_ref=own_ref.at[:, pl.ds(pl.multiple_of((1 - core) * half + chunk * span, 128), span)],
+            dst_ref=pool.at[place, pl.ds(pl.multiple_of((1 - core) * local, 16), local), cols(chunk)],
+            send_sem=mate_send.at[chunk], recv_sem=mate_recv.at[chunk],
+            device_id=(grp, 2 * place + 1 - core), device_id_type=MESH)
+
+    def line_copy(source, way, chunk):
+        to = place + 1 - 2 * way
+        return pltpu.make_async_remote_copy(
+            src_ref=pool.at[source, :, cols(chunk)], dst_ref=pool.at[source, :, cols(chunk)],
+            send_sem=line_send.at[source, way, chunk], recv_sem=line_recv.at[source, chunk],
+            device_id=(grp, 2 * to + core), device_id_type=MESH)
+
+    def has_next(way):
+        return place < columns - 1 if way == 0 else place > 0
+
+    def move_copy(source, group, side, chunk):
+        return pltpu.make_async_remote_copy(
+            src_ref=packed.at[source, pl.ds((group * 2 + side) * rows, rows), cols(chunk)],
+            dst_ref=out_ref.at[
+                pl.ds(pl.multiple_of((grp * columns + source) * rows, 16), rows),
+                pl.ds(pl.multiple_of(core * half + chunk * span, 128), span)],
+            send_sem=move_send.at[source, group, side, chunk],
+            recv_sem=move_recv.at[source, grp, core, chunk],
+            device_id=(group, 2 * place + side), device_id_type=MESH)
+
+    def move_arrival(source, group, side, chunk):
+        return pltpu.make_async_remote_copy(
+            src_ref=packed.at[source, pl.ds(0, rows), cols(chunk)],
+            dst_ref=out_ref.at[
+                pl.ds(pl.multiple_of((group * columns + source) * rows, 16), rows),
+                pl.ds(pl.multiple_of(side * half + chunk * span, 128), span)],
+            send_sem=move_send.at[source, group, side, chunk],
+            recv_sem=move_recv.at[source, group, side, chunk],
+            device_id=(group, 2 * place + side), device_id_type=MESH)
+
+    def stay_copy(source, chunk):
+        return pltpu.make_async_copy(
+            packed.at[source, pl.ds(pl.multiple_of((grp * 2 + core) * rows, 16), rows), cols(chunk)],
+            out_ref.at[
+                pl.ds(pl.multiple_of((grp * columns + source) * rows, 16), rows),
+                pl.ds(pl.multiple_of(core * half + chunk * span, 128), span)],
+            move_recv.at[source, grp, core, chunk])
+
+    for chunk in range(CHUNKS):
+        own_copy(chunk).start()
+        mate_copy(chunk).start()
+    for step in range(1, 2 * columns):
+        mark_copy(step).start()
+    marks[orient] = marks_ref[...]
+
+    def pack(source, chunk):
+        names = jnp.maximum(marks[2 * source], marks[2 * source + 1])[:, : 2 * local]
+        want = 2 * rows * place + lax.broadcasted_iota(jnp.int32, (2 * rows, 2 * local), 0)
+        select = jnp.concatenate(
+            [
+                jnp.where(jnp.broadcast_to(names[g : g + 1], want.shape) == want, 1.0, 0.0)
+                for g in range(groups)
+            ],
+            axis=0,
+        ).astype(jnp.bfloat16)
+
+        @pl.loop(0, span // tile)
+        def _(part):
+            at = pl.ds(pl.multiple_of(chunk * span + part * tile, 128), tile)
+            packed[source, :, at] = jnp.dot(
+                select, pool[source, :, at], preferred_element_type=jnp.float32
+            ).astype(jnp.bfloat16)
+
+        for group in range(groups):
+            for side in range(2):
+                mine = (grp == group) & (core == side)
+
+                @pl.when(mine)
+                def _():
+                    stay_copy(source, chunk).start()
+
+                @pl.when(jnp.logical_not(mine))
+                def _():
+                    move_copy(source, group, side, chunk).start()
+
+    @pl.loop(0, CHUNKS)
+    def _(chunk):
+        own_copy(chunk).wait()
+        mate_arrival(chunk).wait_recv()
+        for way in range(2):
+            @pl.when(has_next(way))
+            def _():
+                line_copy(place, way, chunk).start()
+
+    for step in range(1, 2 * columns):
+        mark_arrival((orient + step) % (2 * columns)).wait_recv()
+
+    @pl.loop(0, CHUNKS)
+    def _(chunk):
+        pack(place, chunk)
+
+    @pl.loop(1, columns)
+    def _(far):
+        @pl.loop(0, CHUNKS)
+        def _(chunk):
+            for way in range(2):
+                source = place - far + 2 * far * way
+
+                @pl.when((source >= 0) & (source < columns))
+                def _():
+                    line_copy(source, way, chunk).wait_recv()
+
+                    @pl.when(has_next(way))
+                    def _():
+                        line_copy(source, way, chunk).start()
+
+                    pack(source, chunk)
+
+    for step in range(1, 2 * columns):
+        mark_copy(step).wait_send()
+
+    @pl.loop(0, CHUNKS)
+    def _(chunk):
+        mate_copy(chunk).wait_send()
+
+        @pl.loop(0, columns)
+        def _(source):
+            for way in range(2):
+                came = source <= place if way == 0 else source >= place
+
+                @pl.when(came & has_next(way))
+                def _():
+                    line_copy(source, way, chunk).wait_send()
+
+            for group in range(groups):
+                for side in range(2):
+                    mine = (grp == group) & (core == side)
+
+                    @pl.when(mine)
+                    def _():
+                        stay_copy(source, chunk).wait()
+
+                    @pl.when(jnp.logical_not(mine))
+                    def _():
+                        move_copy(source, group, side, chunk).wait_send()
+                        move_arrival(source, group, side, chunk).wait_recv()
+
+
+def route(marks, payload, groups, columns, rows):
+    local, width = payload.shape
+    half = width // 2
+    dma = pltpu.SemaphoreType.DMA
+    return pl.pallas_call(
+        functools.partial(route_kernel, groups, columns),
+        out_shape=jax.ShapeDtypeStruct((groups * columns * rows, width), payload.dtype),
+        in_specs=[pl.BlockSpec(memory_space=pltpu.VMEM), pl.BlockSpec(memory_space=pl.ANY)],
+        out_specs=pl.BlockSpec(memory_space=pl.ANY),
+        scratch_shapes=[
+            pltpu.VMEM((columns, 2 * local, half), jnp.bfloat16),
+            pltpu.VMEM((2 * columns,) + marks.shape, jnp.int32),
+            pltpu.VMEM((columns, groups * 2 * rows, half), jnp.bfloat16),
+            dma((CHUNKS,)), dma((CHUNKS,)), dma((CHUNKS,)),
+            dma((2 * columns,)), dma((2 * columns,)),
+            dma((columns, 2, CHUNKS)), dma((columns, CHUNKS)),
+            dma((columns, groups, 2, CHUNKS)), dma((columns, groups, 2, CHUNKS)),
+        ],
+        compiler_params=pltpu.CompilerParams(
+            collective_id=0, has_side_effects=True, vmem_limit_bytes=48 * 2**20
+        ),
+    )(marks, payload)
+
+
+def score_kernel(scale, real_ref, imag_ref, ctf_ref, weight_ref, refs_ref, out_ref):
+    ctf = ctf_ref[...].astype(jnp.float32)
+    tone = weight_ref[...] * ctf
+    power = (tone * ctf).astype(jnp.bfloat16)
+    real = (tone * real_ref[...].astype(jnp.float32)).astype(jnp.bfloat16)
+    imag = (tone * imag_ref[...].astype(jnp.float32)).astype(jnp.bfloat16)
+    ref_real = refs_ref[:, 0, :]
+    ref_imag = refs_ref[:, 1, :]
+    rr, ri = ref_real.astype(jnp.float32), ref_imag.astype(jnp.float32)
+    ref_power = (rr * rr + ri * ri).astype(jnp.bfloat16)
+    contract = (((1,), (1,)), ((), ()))
+    dot = functools.partial(
+        lax.dot_general, dimension_numbers=contract, preferred_element_type=jnp.float32
+    )
+    step = (dot(power, ref_power) - 2.0 * (dot(real, ref_real) + dot(imag, ref_imag))) * scale
+
+    @pl.when(pl.program_id(0) == 0)
+    def _():
+        out_ref[...] = jnp.zeros_like(out_ref)
+
+    out_ref[...] += step
+
+
+def score(arrived, weight, refs, block):
+    slots, width = arrived.shape
+    pixels = width // 3
+    side = pixels // 2 // block
+    wide = refs.shape[0]
+
+    def part(which):
+        return pl.BlockSpec((slots, block), lambda i: (0, i // side * 3 * side + which * side + i % side))
+
+    return pl.pallas_call(
+        functools.partial(score_kernel, 1.0 / math.sqrt(PIX)),
+        grid=(pixels // block,),
+        out_shape=jax.ShapeDtypeStruct((slots, wide), jnp.float32),
+        in_specs=[
+            part(0), part(1), part(2),
+            pl.BlockSpec((1, block), lambda i: (0, i)),
+            pl.BlockSpec((wide, 2, block), lambda i: (0, 0, i)),
+        ],
+        out_specs=pl.BlockSpec((slots, wide), lambda i: (0, 0)),
+        compiler_params=pltpu.CompilerParams(vmem_limit_bytes=48 * 2**20),
+    )(arrived, arrived, arrived, weight, refs)
+
+
+def pick_kernel(slot_ref, table_ref, lists_ref, out_ref, rows_ref):
+    count, entries = lists_ref.shape
+    wide = table_ref.shape[1]
+
+    @pl.loop(0, count)
+    def _(i):
+        rows_ref[pl.ds(i, 1), :] = table_ref[pl.ds(slot_ref[i], 1), :]
+
+    lists = lists_ref[...]
+    place = lists % entries
+    value = jnp.zeros((count, entries), jnp.float32)
+    for b in range(wide // entries):
+        here = jnp.take_along_axis(rows_ref[:, b * entries : (b + 1) * entries], place, axis=1)
+        value = jnp.where(lists // entries == b, here, value)
+    out_ref[...] = value - jnp.mean(value, axis=1, keepdims=True)
+
+
+def pick(slot, table, lists):
+    vmem = pl.BlockSpec(memory_space=pltpu.VMEM)
+    return pl.pallas_call(
+        pick_kernel,
+        out_shape=jax.ShapeDtypeStruct(lists.shape, jnp.float32),
+        in_specs=[pl.BlockSpec(memory_space=pltpu.SMEM), vmem, vmem],
+        out_specs=vmem,
+        scratch_shapes=[pltpu.VMEM((lists.shape[0], table.shape[1]), jnp.float32)],
+    )(slot, table, lists)
+
+
+def per_device_routed(images, ctf, shifts, home, neighbours, references, noise_weight):
+    groups = lax.axis_size("grp")
+    owners = lax.axis_size("orient")
+    local, _, pixels = images.shape
+    slots = max(2, 2 * local // owners)
+    core = lax.axis_index("orient") % 2
+    target = home[:, :, 0]
+    earlier = jnp.arange(local)[None, :] < jnp.arange(local)[:, None]
+    rank = jnp.sum(((target[:, :, None] == target[:, None, :]) & earlier[None]).astype(jnp.int32), axis=2)
+    marks = (target * 2 + core) * slots + rank
+    lane = jnp.arange(128, dtype=jnp.int32)
+    marks = jnp.where(
+        (lane // local == core)[None, :], jnp.tile(marks, (1, 128 // local)), -1
+    )
+    marks = jnp.pad(marks, ((0, -groups % 8), (0, 0)), constant_values=-1)
+    cosine, sine = shift_tables(shifts, BOX)
+    real = images[:, 0].astype(jnp.float32)
+    imag = images[:, 1].astype(jnp.float32)
+    cut = (local, 2, pixels // 2)
+    payload = jnp.stack(
+        [
+            (real * cosine - imag * sine).astype(jnp.bfloat16).reshape(cut),
+            (real * sine + imag * cosine).astype(jnp.bfloat16).reshape(cut),
+            ctf.reshape(cut),
+        ],
+        axis=2,
+    ).reshape(local, 3 * pixels)
+    arrived = route(marks, payload, groups, owners // 2, 2 * slots)
+    table = score(arrived, noise_weight, references[0], 512)
+    returned = lax.all_to_all(
+        table.reshape(groups * owners, slots, -1), ("grp", "orient"), split_axis=0, concat_axis=0, tiled=True
+    )
+    slot = (jnp.arange(groups, dtype=jnp.int32)[:, None] * owners + target) * slots + rank
+    entries = neighbours.shape[2]
+    return pick(
+        slot.T.reshape(-1),
+        returned.reshape(groups * owners * slots, -1),
+        neighbours.reshape(local * groups, entries),
+    ).reshape(neighbours.shape)
+
+
+def per_device(images, ctf, shifts, home, neighbours, references, noise_weight):
+    owners = lax.axis_size("orient")
+    local = images.shape[0]
+    slots = max(2, 2 * local // owners)
+    routed = owners % 2 == 0 and slots % 8 == 0 and local % 16 == 0 and 128 % (2 * local) == 0
+    form = per_device_routed if routed else per_device_plain
+    return form(images, ctf, shifts, home, neighbours, references, noise_weight)
+
+
 def solution(mesh):
     in_specs = (
         P(("grp", "orient"), None, None),

time: 400 us -> 269 us (0.67)
  waiting for transfers between devices: 254 us -> 15.6 us
  Pallas kernels: 0 us -> 223 us
  matrix products: 44.8 us -> 0 us
  local copies, waits for them, and re-layouts: 53.5 us -> 12.7 us
  other arithmetic: 35.9 us -> 13 us
  starting transfers between devices: 10.4 us -> 4.41 us
    all_to_all x2 -> x1, waiting for transfers between devices: 254 us -> 15.6 us  [per_device_routed(): lax.all_to_all(table.reshape(groups * owners, slots, -1), ('grp', 'orient...]
    pallas_call x0 -> x3, Pallas kernels: none -> 223 us  [the longest x1 149 us: route(): pl.pallas_call(functools.partial(route_kernel, groups, columns), out_shap...]
    dot_general x4 -> x0, matrix products: 44.4 us -> none  [the longest x1 16.1 us: pick_columns(): jnp.einsum('ano,ao->an', marks, table, precision=lax.Precision.HIGHEST)]
    unnamed x8, local copies, waits for them, and re-layouts: 37 us -> 0.79 us
    convert_element_type x5 -> x2, other arithmetic: 24.3 us -> 10.3 us  [the longest x1 5.48 us: per_device_routed(): real = images[:, 0].astype(jnp.float32)]
    convert_element_type x2, local copies, waits for them, and re-layouts: 12 us -> 1.78 us  [the longest x1 0.89 us: per_device_routed(): real = images[:, 0].astype(jnp.float32)]
    all_to_all x2 -> x1, starting transfers between devices: 10.4 us -> 4.41 us  [per_device_routed(): lax.all_to_all(table.reshape(groups * owners, slots, -1), ('grp', 'orient...]
    another operation x0 -> x5, local copies, waits for them, and re-layouts: none -> 5.28 us  [the longest x3 5.19 us: per_device_routed(): jnp.stack([(real * cosine - imag * sine).astype(jnp.bfloat16).reshape(cut...]
  transfers between devices with their start and end apart: 2 -> 1, of which waited for: 2 -> 1; matrix products, arithmetic and copies ran while one was open for 9% -> 0% of each run, Pallas kernels for 0% -> 0%
where the time goes in v1:
time: 269 us
  Pallas kernels  223 us (83%)
  waiting for transfers between devices  15.6 us (6%)
  other arithmetic  13 us (5%)
  local copies, waits for them, and re-layouts  12.7 us (5%)
  starting transfers between devices  4.41 us (2%)
    pallas_call x1, Pallas kernels, route(): pl.pallas_call(functools.partial(route_kernel, groups, columns), out_shap...  149 us
    pallas_call x1, Pallas kernels, score(): pl.pallas_call(functools.partial(score_kernel, 1.0 / math.sqrt(PIX)), gri...  70.7 us
    all_to_all x1, waiting for transfers between devices, per_device_routed(): lax.all_to_all(table.reshape(groups * owners, slots, -1), ('grp', 'orient...  15.6 us
    convert_element_type x1, other arithmetic, per_device_routed(): real = images[:, 0].astype(jnp.float32)  5.48 us
  transfers between devices with their start and end apart: 1, of which 1 were waited for; matrix products, arithmetic and copies ran while one was open for 0% of the time, Pallas kernels for 0%

profile of v1, /device:TPU:0, one launch (start us, length us, event | category | flops | bytes accessed | tf_op | source)
XLA Modules:
  0.0 268.6 jit_solution(12019424388427490231)
XLA Ops:
  0.1 0.8 convert_bitcast_fusion.1
  0.8 1.0 convert_reduce_fusion.2
  1.8 0.8 multiply_add_fusion
  2.6 0.1 tile.10
  2.7 0.1 broadcast_in_dim.38
  2.7 0.1 broadcast_in_dim.39
  2.8 0.1 broadcast_in_dim.40
  2.9 1.4 stack_reshape.2
  4.3 1.1 copy.29
  5.4 5.5 %convert_reduce_fusion.1 = (f32[32,8192]{1,0:T(8,128)S(1)}, f32[32,8192]{1,0:T(8,128)S(1)}) fusion(bf16[32,2,8192]{2,1,0:T(2,128)(2,1)S(1)} %copy-done.1), kind=kLoop, calls=%fused_computation.2 | loop fusion | flops 524288 | bytes 3145728 | tf_op jit(solution)/shard_map/convert_element_type | solution.py:407
  10.9 0.9 reshape.212
  11.8 0.9 reshape.213
  12.7 4.9 %subtract_convert_fusion = (bf16[32,2,1,4096]{3,0,2,1:T(8,128)(2,1)S(1)}, bf16[32,2,1,4096]{3,0,2,1:T(8,128)(2,1)S(1)}) fusion(f32[32,2,1,4096]{3,1,0,2:T(2,128)S(1)} %reshape.213, f32[32,2,1,4096]{3,1,0,2:T(2,128)S(1)} %reshape.212, f32[2,4096]{1,0:T(2,128)S(1)} %broadcast_in_dim.40, f32[32]{0:T(128)S(1)} %get-tuple-element.12, ...), kind=kLoop, calls=%fused_computation.4 | loop fusion | flops 3145728 | bytes 3195136 | tf_op jit(solution)/shard_map/convert_element_type | solution.py:412
  17.6 0.2 pad_maximum_fusion
  17.8 2.7 %copy.30 = bf16[32,2,3,4096]{3,2,1,0:T(4,128)(2,1)} copy(bf16[32,2,3,4096]{3,0,2,1:T(8,128)(2,1)S(1)} %pad_maximum_fusion) | data formatting | bytes 3145728 | tf_op jit(solution)/shard_map/stack | solution.py:410
  20.5 3.8 %reshape.207.own_ref = bf16[32,24576]{1,0:T(8,128)(2,1)S(1)} reshape(bf16[32,2,3,4096]{3,2,1,0:T(4,128)(2,1)} %copy.30) | data formatting | bytes 3145728 | tf_op jit(solution)/shard_map/reshape | solution.py:417
  24.3 149.1 %shard_map.73.real_ref.imag_ref.ctf_ref = bf16[256,24576]{1,0:T(8,128)(2,1)} custom-call(s32[8,128]{1,0:T(8,128)S(1)} %pad.4.marks_ref, bf16[32,24576]{1,0:T(8,128)(2,1)S(1)} %reshape.207.own_ref), custom_call_target="tpu_custom_call" | custom-call | tf_op jit(solution)/shard_map/pallas_call | solution.py:297
  173.5 70.7 %shard_map.74 = f32[256,512]{1,0:T(8,128)} custom-call(bf16[256,24576]{1,0:T(8,128)(2,1)} %shard_map.73.real_ref.imag_ref.ctf_ref, bf16[256,24576]{1,0:T(8,128)(2,1)} %shard_map.73.real_ref.imag_ref.ctf_ref, bf16[256,24576]{1,0:T(8,128)(2,1)} %shard_map.73.real_ref.imag_ref.ctf_ref, f32[1,8192]{1,0:T(1,128)S(1)} %copy-done, bf16[512,2,8192]{2,1,0:T(2,128)(2,1)} %bitcast.12), custom_call_target="tpu_custom_call" | custom-call | tf_op jit(solution)/shard_map/pallas_call | solution.py:349
  244.1 4.4 %all-to-all-start = ((f32[32,8,512]{2,1,0:T(8,128)}), f32[32,8,512]{2,1,0:T(8,128)S(1)}, u32[]{:S(2)}, u32[]{:S(2)}) async-start(f32[32,8,512]{2,1,0:T(8,128)} %bitcast.5), calls=%async_computation | async-start | bytes 1048576 | tf_op jit(solution)/shard_map/all_to_all | solution.py:420
  248.5 0.1 copy.24
  248.6 0.7 reshape.206.slot_ref
  249.3 15.6 %all-to-all-done = f32[32,8,512]{2,1,0:T(8,128)S(1)} async-done(((f32[32,8,512]{2,1,0:T(8,128)}), f32[32,8,512]{2,1,0:T(8,128)S(1)}, u32[]{:S(2)}, u32[]{:S(2)}) %all-to-all-start) | async-done | bytes 524320 | tf_op jit(solution)/shard_map/all_to_all | solution.py:420
  264.9 0.8 copy-done.2
  265.7 2.9 %shard_map.75 = f32[128,128]{1,0:T(8,128)} custom-call(s32[128]{0:T(128)} %reshape.206.slot_ref, f32[256,512]{1,0:T(8,128)} %bitcast.13, s32[128,128]{1,0:T(8,128)} %bitcast.14), custom_call_target="tpu_custom_call" | custom-call | tf_op jit(solution)/shard_map/pallas_call | solution.py:382
  (16 shorter events, 0.1 us)
Async XLA Ops:
  0.0 5.4 %copy-start.1 = (bf16[32,2,8192]{2,1,0:T(2,128)(2,1)S(1)}, bf16[32,2,8192]{2,1,0:T(2,128)(2,1)}, u32[]{:S(2)}) copy-start(bf16[32,2,8192]{2,1,0:T(2,128)(2,1)} %param.7) | copy-start | bytes 3145732
  12.7 4.9 %copy-start.3 = (bf16[32,2,1,4096]{3,0,2,1:T(8,128)(2,1)S(1)}, bf16[32,2,1,4096]{3,0,2,1:T(8,128)(2,1)}, u32[]{:S(2)}) copy-start(bf16[32,2,1,4096]{3,0,2,1:T(8,128)(2,1)} %copy.29) | copy-start | bytes 1572868
  24.3 149.2 %copy-start = (f32[1,8192]{1,0:T(1,128)S(1)}, f32[1,8192]{1,0:T(1,128)}, u32[]{:S(2)}) copy-start(f32[1,8192]{1,0:T(1,128)} %weight_ref.1) | copy-start | bytes 98308
  244.1 20.8 %all-to-all-start = ((f32[32,8,512]{2,1,0:T(8,128)}), f32[32,8,512]{2,1,0:T(8,128)S(1)}, u32[]{:S(2)}, u32[]{:S(2)}) async-start(f32[32,8,512]{2,1,0:T(8,128)} %bitcast.5), calls=%async_computation | async-start | bytes 1048576 | tf_op jit(solution)/shard_map/all_to_all | solution.py:420
  264.9 0.8 copy-start.2

commit v2 on v1

--- a/solution.py
+++ b/solution.py
@@ -3,6 +3,7 @@
 
 import jax
 import jax.numpy as jnp
+import numpy as np
 from jax import lax
 from jax.experimental import pallas as pl
 from jax.experimental.pallas import tpu as pltpu
@@ -95,8 +96,8 @@
 CHUNKS = 4
 
 
-def route_kernel(groups, columns, marks_ref, own_ref, out_ref, pool, marks, packed,
-                 own_sem, mate_send, mate_recv, mark_send, mark_recv,
+def route_kernel(groups, columns, marks_ref, own_ref, refs_ref, out_ref, flat_ref, pool, marks, packed,
+                 raw, flat, raw_sem, flat_sem, own_sem, mate_send, mate_recv, mark_send, mark_recv,
                  line_send, line_recv, move_send, move_recv):
     grp = lax.axis_index("grp")
     orient = lax.axis_index("orient")
@@ -190,9 +191,47 @@
                 pl.ds(pl.multiple_of(core * half + chunk * span, 128), span)],
             move_recv.at[source, grp, core, chunk])
 
+    wide, block = flat.shape[2:]
+    tiles = refs_ref.shape[2] // block
+    first = tiles - (columns - 1) * CHUNKS
+
+    def raw_copy(t):
+        at = pl.ds(pl.multiple_of(t * block, 128), block)
+        return pltpu.make_async_copy(refs_ref.at[:, :, at], raw.at[t % 2], raw_sem.at[t % 2])
+
+    def flat_copy(t, which):
+        at = pl.ds(pl.multiple_of((which * tiles + t) * block, 128), block)
+        return pltpu.make_async_copy(flat.at[t % 2, which], flat_ref.at[:, at], flat_sem.at[t % 2, which])
+
+    def lay_out(t):
+        raw_copy(t).wait()
+
+        @pl.when(t + 1 < tiles)
+        def _():
+            raw_copy(t + 1).start()
+
+        @pl.when(t >= 2)
+        def _():
+            for which in range(3):
+                flat_copy(t - 2, which).wait()
+
+        @pl.loop(0, wide // 32)
+        def _(r):
+            at = pl.ds(pl.multiple_of(r * 32, 32), 32)
+            real = raw[t % 2, at, 0, :]
+            imag = raw[t % 2, at, 1, :]
+            rf, mf = real.astype(jnp.float32), imag.astype(jnp.float32)
+            flat[t % 2, 0, at, :] = real
+            flat[t % 2, 1, at, :] = imag
+            flat[t % 2, 2, at, :] = (rf * rf + mf * mf).astype(jnp.bfloat16)
+
+        for which in range(3):
+            flat_copy(t, which).start()
+
     for chunk in range(CHUNKS):
         own_copy(chunk).start()
         mate_copy(chunk).start()
+    raw_copy(0).start()
     for step in range(1, 2 * columns):
         mark_copy(step).start()
     marks[orient] = marks_ref[...]
@@ -243,6 +282,10 @@
     def _(chunk):
         pack(place, chunk)
 
+    @pl.loop(0, first)
+    def _(t):
+        lay_out(t)
+
     @pl.loop(1, columns)
     def _(far):
         @pl.loop(0, CHUNKS)
@@ -260,6 +303,12 @@
 
                     pack(source, chunk)
 
+            lay_out(first + (far - 1) * CHUNKS + chunk)
+
+    for t in (tiles - 2, tiles - 1):
+        for which in range(3):
+            flat_copy(t, which).wait()
+
     for step in range(1, 2 * columns):
         mark_copy(step).wait_send()
 
@@ -290,19 +339,72 @@
                         move_arrival(source, group, side, chunk).wait_recv()
 
 
-def route(marks, payload, groups, columns, rows):
+def shift_kernel(shifts_ref, turn_ref, images_ref, ctf_ref, out_ref):
+    local, pixels = ctf_ref.shape
+    half = pixels // 2
+    lanes = turn_ref.shape[1]
+    side = BOX // 2
+    cosine = jnp.broadcast_to(turn_ref[0:1], (local, lanes))
+    sine = jnp.broadcast_to(turn_ref[1:2], (local, lanes))
+    move_x, move_y = shifts_ref[:, 0:1], shifts_ref[:, 1:2]
+    lane = lax.broadcasted_iota(jnp.int32, (local, lanes), 1)
+    base = move_x * (lane % side) + move_y * (lane // side)
+
+    @pl.loop(0, pixels // lanes)
+    def _(piece):
+        at = pl.ds(pl.multiple_of(piece * lanes, lanes), lanes)
+        steps = (base + move_y * (piece * (lanes // side))) & (BOX - 1)
+        c = jnp.take_along_axis(cosine, steps, axis=1)
+        s = jnp.take_along_axis(sine, steps, axis=1)
+        real = images_ref[:, 0, at].astype(jnp.float32)
+        imag = images_ref[:, 1, at].astype(jnp.float32)
+        start = piece * lanes + piece // (half // lanes) * 2 * half
+
+        def put(which, value):
+            to = pl.ds(pl.multiple_of(start + which * half, lanes), lanes)
+            out_ref[:, to] = value
+
+        put(0, (real * c - imag * s).astype(jnp.bfloat16))
+        put(1, (real * s + imag * c).astype(jnp.bfloat16))
+        put(2, ctf_ref[:, at])
+
+
+def shift(images, ctf, shifts):
+    local, _, pixels = images.shape
+    angle = -2.0 * np.pi / BOX * np.arange(BOX)
+    turn = np.zeros((8, BOX), np.float32)
+    turn[0], turn[1] = np.cos(angle), np.sin(angle)
+    vmem = pl.BlockSpec(memory_space=pltpu.VMEM)
+    return pl.pallas_call(
+        shift_kernel,
+        out_shape=jax.ShapeDtypeStruct((local, 3 * pixels), jnp.bfloat16),
+        in_specs=[vmem] * 4,
+        out_specs=vmem,
+        compiler_params=pltpu.CompilerParams(vmem_limit_bytes=32 * 2**20),
+    )(shifts, jnp.asarray(turn), images, ctf)
+
+
+def route(marks, payload, refs, groups, columns, rows):
     local, width = payload.shape
+    wide, _, pixels = refs.shape
+    block = 512
     half = width // 2
     dma = pltpu.SemaphoreType.DMA
     return pl.pallas_call(
         functools.partial(route_kernel, groups, columns),
-        out_shape=jax.ShapeDtypeStruct((groups * columns * rows, width), payload.dtype),
-        in_specs=[pl.BlockSpec(memory_space=pltpu.VMEM), pl.BlockSpec(memory_space=pl.ANY)],
-        out_specs=pl.BlockSpec(memory_space=pl.ANY),
+        out_shape=(
+            jax.ShapeDtypeStruct((groups * columns * rows, width), payload.dtype),
+            jax.ShapeDtypeStruct((wide, 3 * pixels), refs.dtype),
+        ),
+        in_specs=[pl.BlockSpec(memory_space=pltpu.VMEM)] + [pl.BlockSpec(memory_space=pl.ANY)] * 2,
+        out_specs=(pl.BlockSpec(memory_space=pl.ANY), pl.BlockSpec(memory_space=pl.ANY)),
         scratch_shapes=[
             pltpu.VMEM((columns, 2 * local, half), jnp.bfloat16),
             pltpu.VMEM((2 * columns,) + marks.shape, jnp.int32),
             pltpu.VMEM((columns, groups * 2 * rows, half), jnp.bfloat16),
+            pltpu.VMEM((2, wide, 2, block), refs.dtype),
+            pltpu.VMEM((2, 3, wide, block), refs.dtype),
+            dma((2,)), dma((2, 3)),
             dma((CHUNKS,)), dma((CHUNKS,)), dma((CHUNKS,)),
             dma((2 * columns,)), dma((2 * columns,)),
             dma((columns, 2, CHUNKS)), dma((columns, CHUNKS)),
@@ -311,24 +413,22 @@
         compiler_params=pltpu.CompilerParams(
             collective_id=0, has_side_effects=True, vmem_limit_bytes=48 * 2**20
         ),
-    )(marks, payload)
-
-
-def score_kernel(scale, real_ref, imag_ref, ctf_ref, weight_ref, refs_ref, out_ref):
+    )(marks, payload, refs)
+
+
+def score_kernel(scale, real_ref, imag_ref, ctf_ref, weight_ref, ref_real, ref_imag, ref_power, out_ref):
     ctf = ctf_ref[...].astype(jnp.float32)
     tone = weight_ref[...] * ctf
     power = (tone * ctf).astype(jnp.bfloat16)
     real = (tone * real_ref[...].astype(jnp.float32)).astype(jnp.bfloat16)
     imag = (tone * imag_ref[...].astype(jnp.float32)).astype(jnp.bfloat16)
-    ref_real = refs_ref[:, 0, :]
-    ref_imag = refs_ref[:, 1, :]
-    rr, ri = ref_real.astype(jnp.float32), ref_imag.astype(jnp.float32)
-    ref_power = (rr * rr + ri * ri).astype(jnp.bfloat16)
     contract = (((1,), (1,)), ((), ()))
     dot = functools.partial(
         lax.dot_general, dimension_numbers=contract, preferred_element_type=jnp.float32
     )
-    step = (dot(power, ref_power) - 2.0 * (dot(real, ref_real) + dot(imag, ref_imag))) * scale
+    step = (
+        dot(power, ref_power[...]) - 2.0 * (dot(real, ref_real[...]) + dot(imag, ref_imag[...]))
+    ) * scale
 
     @pl.when(pl.program_id(0) == 0)
     def _():
@@ -345,6 +445,9 @@
 
     def part(which):
         return pl.BlockSpec((slots, block), lambda i: (0, i // side * 3 * side + which * side + i % side))
+
+    def known(which):
+        return pl.BlockSpec((wide, block), lambda i: (0, which * 2 * side + i))
 
     return pl.pallas_call(
         functools.partial(score_kernel, 1.0 / math.sqrt(PIX)),
@@ -353,11 +456,11 @@
         in_specs=[
             part(0), part(1), part(2),
             pl.BlockSpec((1, block), lambda i: (0, i)),
-            pl.BlockSpec((wide, 2, block), lambda i: (0, 0, i)),
+            known(0), known(1), known(2),
         ],
         out_specs=pl.BlockSpec((slots, wide), lambda i: (0, 0)),
         compiler_params=pltpu.CompilerParams(vmem_limit_bytes=48 * 2**20),
-    )(arrived, arrived, arrived, weight, refs)
+    )(arrived, arrived, arrived, weight, refs, refs, refs)
 
 
 def pick_kernel(slot_ref, table_ref, lists_ref, out_ref, rows_ref):
@@ -403,20 +506,9 @@
         (lane // local == core)[None, :], jnp.tile(marks, (1, 128 // local)), -1
     )
     marks = jnp.pad(marks, ((0, -groups % 8), (0, 0)), constant_values=-1)
-    cosine, sine = shift_tables(shifts, BOX)
-    real = images[:, 0].astype(jnp.float32)
-    imag = images[:, 1].astype(jnp.float32)
-    cut = (local, 2, pixels // 2)
-    payload = jnp.stack(
-        [
-            (real * cosine - imag * sine).astype(jnp.bfloat16).reshape(cut),
-            (real * sine + imag * cosine).astype(jnp.bfloat16).reshape(cut),
-            ctf.reshape(cut),
-        ],
-        axis=2,
-    ).reshape(local, 3 * pixels)
-    arrived = route(marks, payload, groups, owners // 2, 2 * slots)
-    table = score(arrived, noise_weight, references[0], 512)
+    payload = shift(images, ctf, shifts)
+    arrived, flat = route(marks, payload, references[0], groups, owners // 2, 2 * slots)
+    table = score(arrived, noise_weight, flat, 1024)
     returned = lax.all_to_all(
         table.reshape(groups * owners, slots, -1), ("grp", "orient"), split_axis=0, concat_axis=0, tiled=True
     )
@@ -433,7 +525,9 @@
     owners = lax.axis_size("orient")
     local = images.shape[0]
     slots = max(2, 2 * local // owners)
-    routed = owners % 2 == 0 and slots % 8 == 0 and local % 16 == 0 and 128 % (2 * local) == 0
+    parts = images.shape[2] // 512
+    long = parts >= (owners // 2 - 1) * CHUNKS and images.shape[2] % 2048 == 0
+    routed = long and owners % 2 == 0 and slots % 8 == 0 and local % 16 == 0 and 128 % (2 * local) == 0
     form = per_device_routed if routed else per_device_plain
     return form(images, ctf, shifts, home, neighbours, references, noise_weight)
 

time: 269 us -> 207 us (0.77)
  Pallas kernels: 223 us -> 180 us
  other arithmetic: 13 us -> 1.75 us
  local copies, waits for them, and re-layouts: 12.7 us -> 5.3 us
    pallas_call x1, Pallas kernels: 70.7 us -> 16.6 us  [score(): pl.pallas_call(functools.partial(score_kernel, 1.0 / math.sqrt(PIX)), gri...]
    pallas_call x0 -> x1, Pallas kernels: none -> 10.8 us  [shift(): pl.pallas_call(shift_kernel, out_shape=jax.ShapeDtypeStruct((local, 3 * p...]
    convert_element_type x4 -> x0, other arithmetic: 10.3 us -> none  [the longest x1 5.48 us: per_device_routed(): real = images[:, 0].astype(jnp.float32)]
    another operation x3 -> x0, local copies, waits for them, and re-layouts: 5.19 us -> none  [per_device_routed(): jnp.stack([(real * cosine - imag * sine).astype(jnp.bfloat16).reshape(cut...]
    reshape x1 -> x0, local copies, waits for them, and re-layouts: 3.81 us -> none  [per_device_routed(): payload = jnp.stack([(real * cosine - imag * sine).astype(jnp.bfloat16).r...]
    unnamed x8 -> x11, local copies, waits for them, and re-layouts: 0.79 us -> 4.5 us
where the time goes in v2:
time: 207 us
  Pallas kernels  180 us (87%)
  waiting for transfers between devices  15.7 us (8%)
  local copies, waits for them, and re-layouts  5.3 us (3%)
  starting transfers between devices  4.41 us (2%)
    pallas_call x1, Pallas kernels, route(): pl.pallas_call(functools.partial(route_kernel, groups, columns), out_shap...  149 us
    pallas_call x1, Pallas kernels, score(): pl.pallas_call(functools.partial(score_kernel, 1.0 / math.sqrt(PIX)), gri...  16.6 us
    all_to_all x1, waiting for transfers between devices, per_device_routed(): lax.all_to_all(table.reshape(groups * owners, slots, -1), ('grp', 'orient...  15.7 us
    pallas_call x1, Pallas kernels, shift(): pl.pallas_call(shift_kernel, out_shape=jax.ShapeDtypeStruct((local, 3 * p...  10.8 us
    unnamed x11, local copies, waits for them, and re-layouts  4.5 us
    all_to_all x1, starting transfers between devices, per_device_routed(): lax.all_to_all(table.reshape(groups * owners, slots, -1), ('grp', 'orient...  4.41 us
  transfers between devices with their start and end apart: 1, of which 1 were waited for; matrix products, arithmetic and copies ran while one was open for 0% of the time, Pallas kernels for 0%

profile of v2, /device:TPU:0, one launch (start us, length us, event | category | flops | bytes accessed | tf_op | source)
XLA Modules:
  0.0 206.7 jit_solution(13096454936070296225)
XLA Ops:
  0.0 0.0 copy-start.2
  0.0 1.0 convert_reduce_fusion
  1.0 0.8 multiply_add_fusion
  1.8 0.1 tile.10
  1.9 0.8 copy.14.shifts_ref
  2.6 0.0 copy-start
  2.6 1.2 copy-done
  3.9 0.0 copy-start.1
  3.9 1.0 copy-done.1
  4.9 0.0 copy-start.3
  4.9 0.7 copy-done.3
  5.6 10.8 %shard_map.82.own_ref = bf16[32,24576]{1,0:T(8,128)(2,1)S(1)} custom-call(s32[32,2]{1,0:T(8,128)S(1)} %copy.14.shifts_ref, f32[8,128]{1,0:T(8,128)S(1)} %copy-done.3, bf16[32,2,8192]{2,1,0:T(2,128)(2,1)S(1)} %copy-done, bf16[32,8192]{1,0:T(8,128)(2,1)S(1)} %copy-done.1), custom_call_target="tpu_custom_call" | custom-call | tf_op jit(solution)/shard_map/pallas_call | solution.py:378
  16.4 149.2 %shard_map.83 = (bf16[256,24576]{1,0:T(8,128)(2,1)}, bf16[512,24576]{1,0:T(8,128)(2,1)}) custom-call(s32[8,128]{1,0:T(8,128)S(1)} %pad.4.marks_ref, bf16[32,24576]{1,0:T(8,128)(2,1)S(1)} %shard_map.82.own_ref, bf16[512,2,8192]{2,1,0:T(2,128)(2,1)} %bitcast.8), custom_call_target="tpu_custom_call" | custom-call | tf_op jit(solution)/shard_map/pallas_call | solution.py:393
  165.6 0.0 copy-done.2
  165.6 16.6 %shard_map.84 = f32[256,512]{1,0:T(8,128)} custom-call(bf16[256,24576]{1,0:T(8,128)(2,1)} %get-tuple-element.7.real_ref.imag_ref.ctf_ref, bf16[256,24576]{1,0:T(8,128)(2,1)} %get-tuple-element.7.real_ref.imag_ref.ctf_ref, bf16[256,24576]{1,0:T(8,128)(2,1)} %get-tuple-element.7.real_ref.imag_ref.ctf_ref, f32[1,8192]{1,0:T(1,128)S(1)} %copy-done.2, ...), custom_call_target="tpu_custom_call" | custom-call | tf_op jit(solution)/shard_map/pallas_call | solution.py:452
  182.3 4.4 %all-to-all-start = ((f32[32,8,512]{2,1,0:T(8,128)}), f32[32,8,512]{2,1,0:T(8,128)S(1)}, u32[]{:S(2)}, u32[]{:S(2)}) async-start(f32[32,8,512]{2,1,0:T(8,128)} %bitcast.3), calls=%async_computation | async-start | bytes 1048576 | tf_op jit(solution)/shard_map/all_to_all | solution.py:512
  186.7 0.1 copy.13
  186.8 0.6 reshape.60.slot_ref
  187.4 15.7 %all-to-all-done = f32[32,8,512]{2,1,0:T(8,128)S(1)} async-done(((f32[32,8,512]{2,1,0:T(8,128)}), f32[32,8,512]{2,1,0:T(8,128)S(1)}, u32[]{:S(2)}, u32[]{:S(2)}) %all-to-all-start) | async-done | bytes 524320 | tf_op jit(solution)/shard_map/all_to_all | solution.py:512
  203.1 0.0 copy-start.4
  203.1 0.8 copy-done.4
  203.8 2.9 %shard_map.85 = f32[128,128]{1,0:T(8,128)} custom-call(s32[128]{0:T(128)} %reshape.60.slot_ref, f32[256,512]{1,0:T(8,128)} %bitcast.9, s32[128,128]{1,0:T(8,128)} %bitcast.10), custom_call_target="tpu_custom_call" | custom-call | tf_op jit(solution)/shard_map/pallas_call | solution.py:485
  (6 shorter events, 0.0 us)
Async XLA Ops:
  0.0 165.6 %copy-start.2 = (f32[1,8192]{1,0:T(1,128)S(1)}, f32[1,8192]{1,0:T(1,128)}, u32[]{:S(2)}) copy-start(f32[1,8192]{1,0:T(1,128)} %weight_ref.1) | copy-start | bytes 98308
  2.6 1.2 copy-start
  3.9 1.0 copy-start.1
  4.9 0.7 copy-start.3
  182.3 20.8 %all-to-all-start = ((f32[32,8,512]{2,1,0:T(8,128)}), f32[32,8,512]{2,1,0:T(8,128)S(1)}, u32[]{:S(2)}, u32[]{:S(2)}) async-start(f32[32,8,512]{2,1,0:T(8,128)} %bitcast.3), calls=%async_computation | async-start | bytes 1048576 | tf_op jit(solution)/shard_map/all_to_all | solution.py:512
  203.1 0.8 copy-start.4

commit v3 on v2

--- a/solution.py
+++ b/solution.py
@@ -165,7 +165,7 @@
 
     def move_copy(source, group, side, chunk):
         return pltpu.make_async_remote_copy(
-            src_ref=packed.at[source, pl.ds((group * 2 + side) * rows, rows), cols(chunk)],
+            src_ref=packed.at[source, pl.ds(pl.multiple_of((group * 2 + side) * rows, 16), rows), cols(chunk)],
             dst_ref=out_ref.at[
                 pl.ds(pl.multiple_of((grp * columns + source) * rows, 16), rows),
                 pl.ds(pl.multiple_of(core * half + chunk * span, 128), span)],
@@ -254,17 +254,11 @@
                 select, pool[source, :, at], preferred_element_type=jnp.float32
             ).astype(jnp.bfloat16)
 
-        for group in range(groups):
+        for step in list(range(1, groups, 2)) + list(range(2, groups, 2)):
             for side in range(2):
-                mine = (grp == group) & (core == side)
-
-                @pl.when(mine)
-                def _():
-                    stay_copy(source, chunk).start()
-
-                @pl.when(jnp.logical_not(mine))
-                def _():
-                    move_copy(source, group, side, chunk).start()
+                move_copy(source, (grp + step) % groups, side, chunk).start()
+        move_copy(source, grp, 1 - core, chunk).start()
+        stay_copy(source, chunk).start()
 
     @pl.loop(0, CHUNKS)
     def _(chunk):
@@ -350,7 +344,7 @@
     lane = lax.broadcasted_iota(jnp.int32, (local, lanes), 1)
     base = move_x * (lane % side) + move_y * (lane // side)
 
-    @pl.loop(0, pixels // lanes)
+    @pl.loop(0, pixels // lanes, unroll=8)
     def _(piece):
         at = pl.ds(pl.multiple_of(piece * lanes, lanes), lanes)
         steps = (base + move_y * (piece * (lanes // side))) & (BOX - 1)

time: 207 us -> 200 us (0.966)
  Pallas kernels: 180 us -> 172 us
    pallas_call x1, Pallas kernels: 10.8 us -> 3.58 us  [shift(): pl.pallas_call(shift_kernel, out_shape=jax.ShapeDtypeStruct((local, 3 * p...]
where the time goes in v3:
time: 200 us; the launch traced here: 199 us
  Pallas kernels  172 us (86%)
  waiting for transfers between devices  15.7 us (8%)
  local copies, waits for them, and re-layouts  5.3 us (3%)
  starting transfers between devices  4.41 us (2%)
    pallas_call x1, Pallas kernels, route(): pl.pallas_call(functools.partial(route_kernel, groups, columns), out_shap...  149 us
    pallas_call x1, Pallas kernels, score(): pl.pallas_call(functools.partial(score_kernel, 1.0 / math.sqrt(PIX)), gri...  16.7 us
    all_to_all x1, waiting for transfers between devices, per_device_routed(): lax.all_to_all(table.reshape(groups * owners, slots, -1), ('grp', 'orient...  15.7 us
    unnamed x11, local copies, waits for them, and re-layouts  4.5 us
    all_to_all x1, starting transfers between devices, per_device_routed(): lax.all_to_all(table.reshape(groups * owners, slots, -1), ('grp', 'orient...  4.41 us
  transfers between devices with their start and end apart: 1, of which 1 were waited for; matrix products, arithmetic and copies ran while one was open for 0% of the time, Pallas kernels for 0%

profile of v3, /device:TPU:0, one launch (start us, length us, event | category | flops | bytes accessed | tf_op | source)
XLA Modules:
  0.0 199.5 jit_solution(13118630805584671017)
XLA Ops:
  0.0 0.0 copy-start.2
  0.0 1.0 convert_reduce_fusion
  1.0 0.8 multiply_add_fusion
  1.8 0.1 tile.10
  1.9 0.8 copy.14.shifts_ref
  2.6 0.0 copy-start
  2.6 1.2 copy-done
  3.9 0.0 copy-start.1
  3.9 1.0 copy-done.1
  4.9 0.0 copy-start.3
  4.9 0.7 copy-done.3
  5.6 3.6 %shard_map.82.own_ref = bf16[32,24576]{1,0:T(8,128)(2,1)S(1)} custom-call(s32[32,2]{1,0:T(8,128)S(1)} %copy.14.shifts_ref, f32[8,128]{1,0:T(8,128)S(1)} %copy-done.3, bf16[32,2,8192]{2,1,0:T(2,128)(2,1)S(1)} %copy-done, bf16[32,8192]{1,0:T(8,128)(2,1)S(1)} %copy-done.1), custom_call_target="tpu_custom_call" | custom-call | tf_op jit(solution)/shard_map/pallas_call | solution.py:372
  9.2 149.2 %shard_map.83 = (bf16[256,24576]{1,0:T(8,128)(2,1)}, bf16[512,24576]{1,0:T(8,128)(2,1)}) custom-call(s32[8,128]{1,0:T(8,128)S(1)} %pad.4.marks_ref, bf16[32,24576]{1,0:T(8,128)(2,1)S(1)} %shard_map.82.own_ref, bf16[512,2,8192]{2,1,0:T(2,128)(2,1)} %bitcast.8), custom_call_target="tpu_custom_call" | custom-call | tf_op jit(solution)/shard_map/pallas_call | solution.py:387
  158.4 0.0 copy-done.2
  158.4 16.7 %shard_map.84 = f32[256,512]{1,0:T(8,128)} custom-call(bf16[256,24576]{1,0:T(8,128)(2,1)} %get-tuple-element.7.real_ref.imag_ref.ctf_ref, bf16[256,24576]{1,0:T(8,128)(2,1)} %get-tuple-element.7.real_ref.imag_ref.ctf_ref, bf16[256,24576]{1,0:T(8,128)(2,1)} %get-tuple-element.7.real_ref.imag_ref.ctf_ref, f32[1,8192]{1,0:T(1,128)S(1)} %copy-done.2, ...), custom_call_target="tpu_custom_call" | custom-call | tf_op jit(solution)/shard_map/pallas_call | solution.py:446
  175.0 4.4 %all-to-all-start = ((f32[32,8,512]{2,1,0:T(8,128)}), f32[32,8,512]{2,1,0:T(8,128)S(1)}, u32[]{:S(2)}, u32[]{:S(2)}) async-start(f32[32,8,512]{2,1,0:T(8,128)} %bitcast.3), calls=%async_computation | async-start | bytes 1048576 | tf_op jit(solution)/shard_map/all_to_all | solution.py:506
  179.5 0.1 copy.13
  179.5 0.6 reshape.60.slot_ref
  180.2 15.7 %all-to-all-done = f32[32,8,512]{2,1,0:T(8,128)S(1)} async-done(((f32[32,8,512]{2,1,0:T(8,128)}), f32[32,8,512]{2,1,0:T(8,128)S(1)}, u32[]{:S(2)}, u32[]{:S(2)}) %all-to-all-start) | async-done | bytes 524320 | tf_op jit(solution)/shard_map/all_to_all | solution.py:506
  195.8 0.0 copy-start.4
  195.8 0.8 copy-done.4
  196.6 2.9 %shard_map.85 = f32[128,128]{1,0:T(8,128)} custom-call(s32[128]{0:T(128)} %reshape.60.slot_ref, f32[256,512]{1,0:T(8,128)} %bitcast.9, s32[128,128]{1,0:T(8,128)} %bitcast.10), custom_call_target="tpu_custom_call" | custom-call | tf_op jit(solution)/shard_map/pallas_call | solution.py:479
  (6 shorter events, 0.0 us)
Async XLA Ops:
  0.0 158.4 %copy-start.2 = (f32[1,8192]{1,0:T(1,128)S(1)}, f32[1,8192]{1,0:T(1,128)}, u32[]{:S(2)}) copy-start(f32[1,8192]{1,0:T(1,128)} %weight_ref.1) | copy-start | bytes 98308
  2.6 1.2 copy-start
  3.9 1.0 copy-start.1
  4.9 0.7 copy-start.3
  175.0 20.8 %all-to-all-start = ((f32[32,8,512]{2,1,0:T(8,128)}), f32[32,8,512]{2,1,0:T(8,128)S(1)}, u32[]{:S(2)}, u32[]{:S(2)}) async-start(f32[32,8,512]{2,1,0:T(8,128)} %bitcast.3), calls=%async_computation | async-start | bytes 1048576 | tf_op jit(solution)/shard_map/all_to_all | solution.py:506
  195.8 0.8 copy-start.4
